TPU v7x, 32 devices: a whole 2x2x4 slice. The times are simulated.
32 devices in a mesh: groups: 2 (over x), tensor: 16 (over z, y, core).
Axes of the slice: x: 2, y: 2, z: 4, core: 2. Of those that a mesh axis runs over, the one named last changes fastest.
Arguments:
- tokens: bfloat16 [256, 8192], P(('groups', 'tensor')), parts along dimension 0, may hold values from -6 to 6
- gate_matrix: bfloat16 [8192, 14336], P(None, 'tensor'), may hold values from -0.0625 to 0.0625
- up_matrix: bfloat16 [8192, 14336], P(None, 'tensor'), may hold values from -0.0625 to 0.0625
- adapter_input_maps: bfloat16 [16, 8192, 128], P('tensor'), may hold values from -0.0625 to 0.0625
- adapter_output_maps: bfloat16 [16, 2, 64, 14336], P(None, None, None, 'tensor'), may hold values from -0.75 to 0.75
- request_adapter: int32 [64, 1], P(('groups', 'tensor')), parts along dimension 0, may hold values from 0 to 15; in each aligned block of 32 rows (0 to 31, 32 to 63, ...) at most 8 rows name the same one
Outputs:
- hidden: bfloat16 [256, 14336], P('groups', 'tensor'), parts along dimension 0
There are 2 independent parts, one for each index of `groups`. A program takes and returns all parts, laid end to end along the dimension named above; an argument that names none is the same for every part. Nothing has to cross between parts.
Inputs may be any that keep to these rules, and one draw needn't show every extreme that they name: `request_adapter`: no adapter is named by more than 8 requests, a bound that some block reaches; every adapter is named by some request.
All inputs are finite; a program needn't handle non-finite values.
Results may differ from a plain program's by a relative error of at most 0.0054.
Values may be sent and summed in bfloat16 or wider, within the bound.
A program may use at most 128 MiB of HBM per device.

v0:
```python
import jax
import jax.numpy as jnp
from jax import lax
from jax.sharding import PartitionSpec as P

SEQ = 4
MOST = 8


def slot_rows(adapter_table, count):
    n_requests = adapter_table.shape[0]
    match = adapter_table[None, :] == jnp.arange(count, dtype=jnp.int32)[:, None]
    order = jnp.cumsum(match.astype(jnp.int32), axis=1) - 1
    picks = match[:, None, :] & (
        order[:, None, :] == jnp.arange(MOST, dtype=jnp.int32)[None, :, None]
    )
    requests = jnp.sum(
        jnp.where(picks, jnp.arange(n_requests, dtype=jnp.int32)[None, None, :], 0), axis=2
    )
    filled = jnp.any(picks, axis=2)
    token_rows = (
        requests[:, :, None] * SEQ + jnp.arange(SEQ, dtype=jnp.int32)[None, None, :]
    ).reshape(count, MOST * SEQ)
    live = jnp.repeat(filled, SEQ, axis=1)
    return (token_rows, live)


def local(tokens, gate_matrix, up_matrix, adapter_input_maps, adapter_output_maps, request_adapter):
    hidden_local = gate_matrix.shape[1]
    reduced_width = adapter_input_maps.shape[2]
    rank = reduced_width // 2
    kept_adapters = adapter_input_maps.shape[0]
    device = lax.axis_index("tensor")
    adapter_table = lax.all_gather(request_adapter, "tensor", axis=0, tiled=True)[:, 0]
    n_requests = adapter_table.shape[0]
    total_rows = n_requests * SEQ
    count = kept_adapters * lax.axis_size("tensor")
    token_rows, live = slot_rows(adapter_table, count)
    local_token_rows = lax.dynamic_slice_in_dim(
        token_rows, device * kept_adapters, kept_adapters, 0
    )
    own_live = lax.dynamic_slice_in_dim(live, device * kept_adapters, kept_adapters, 0)
    collected_rows = lax.all_gather(tokens, "tensor", axis=0, tiled=True)
    gate_plain = jnp.dot(collected_rows, gate_matrix, preferred_element_type=jnp.float32)
    up_plain = jnp.dot(collected_rows, up_matrix, preferred_element_type=jnp.float32)
    compact = jnp.stack(
        [
            jnp.where(
                own_live[0][:, None],
                jnp.dot(
                    collected_rows[local_token_rows[0]],
                    adapter_input_maps[0],
                    preferred_element_type=jnp.float32,
                ),
                0.0,
            )
        ]
    )
    dense = (
        jnp.zeros((total_rows, reduced_width), jnp.float32)
        .at[local_token_rows.reshape(-1)]
        .add(compact.reshape(-1, reduced_width))
    )
    reduced_rank = lax.psum(dense, "tensor").astype(jnp.bfloat16)
    slotted = jnp.where(live[:, :, None], reduced_rank[token_rows], jnp.zeros((), jnp.bfloat16))
    slot_count = slotted.shape[1]
    slotted_reduced = slotted.reshape(count, slot_count, 2, rank)
    slot_terms = jnp.einsum(
        "xbyd,xydv->xbyv", slotted_reduced, adapter_output_maps, preferred_element_type=jnp.float32
    )
    slot_terms = jnp.where(live[:, :, None, None], slot_terms, 0.0).reshape(
        count * slot_count, 2 * hidden_local
    )
    adapter_terms = (
        jnp.zeros((total_rows, 2 * hidden_local), jnp.float32)
        .at[token_rows.reshape(-1)]
        .add(slot_terms)
    )
    gate_output = gate_plain + adapter_terms[:, :hidden_local]
    up_output = up_plain + adapter_terms[:, hidden_local:]
    return (jax.nn.silu(gate_output) * up_output).astype(jnp.bfloat16)


def solution(mesh):
    in_specs = (
        P(("groups", "tensor"), None),
        P(None, "tensor"),
        P(None, "tensor"),
        P("tensor", None, None),
        P(None, None, None, "tensor"),
        P(("groups", "tensor"), None),
    )
    out_specs = P("groups", "tensor")
    return jax.shard_map(local, mesh=mesh, in_specs=in_specs, out_specs=out_specs, check_vma=False)
```

profile of v0, /device:TPU:0, one launch (start us, length us, event | category | flops | bytes accessed | tf_op | source)
XLA Modules:
  0.0 158.4 jit_solution(14899655708848629975)
XLA Ops:
  6.5 0.7 all-gather.2.cloned.1.call-update
  7.4 1.2 dynamic-slice
  9.3 0.8 bitcast_dynamic-update-slice_fusion
  10.0 13.7 %all-reduce = s32[32]{0:T(128)S(1)} all-reduce(s32[32]{0:T(128)S(1)} %bitcast_dynamic-update-slice_fusion), channel_id=1, replica_groups=mesh['groups'=2,'tensor'=16] {'tensor'}, use_global_device_ids=true, to_apply=%add | all-reduce | flops 32 | bytes 256
  23.8 0.2 reduce_window_sum.11
  24.0 0.4 select_reduce_fusion
  24.4 0.4 fusion.12
  25.2 0.1 copy.29
  25.3 0.1 add.117
  25.4 0.2 dynamic-slice_reduce_fusion
  25.6 0.2 fusion.15
  25.8 27.8 %all-gather.2.cloned.1.call-done = bf16[128,8192]{1,0:T(8,128)(2,1)} async-done(((bf16[8,8192]{1,0:T(8,128)(2,1)}), bf16[128,8192]{1,0:T(8,128)(2,1)}) %all-gather.2.cloned.1.call-update) | async-done | bytes 2097168 | tf_op jit(solution)/shard_map/all_gather | solution.py:43
  53.6 3.2 %gather_fusion = bf16[32,8192]{1,0:T(8,128)(2,1)S(1)} fusion(bf16[128,8192]{1,0:T(8,128)(2,1)} %all-gather.2.cloned.1.call-done, s32[1024]{0:T(1024)S(1)} %pad_clamp_fusion.1), kind=kCustom, calls=%fused_computation | custom fusion | bytes 1048704 | tf_op jit(solution)/shard_map/gather | solution.py:51
  56.8 0.4 fusion.4
  57.3 0.7 scatter_custom_fusion
  58.0 59.6 %psum.7 = bf16[128,128]{1,0:T(8,128)(2,1)S(1)} all-reduce(f32[128,128]{1,0:T(8,128)S(1)} %scatter_custom_fusion), channel_id=1, replica_groups=mesh['groups'=2,'tensor'=16] {'tensor'}, use_global_device_ids=true, to_apply=%region_4.5 | all-reduce | flops 16384 | bytes 98304 | tf_op jit(solution)/shard_map/psum | solution.py:64
  117.6 1.3 gather_fusion.1
  118.9 0.1 gather.10
  119.0 2.8 %select_bitcast_fusion = f32[16,32,2,896]{3,1,2,0:T(8,128)S(1)} fusion(bf16[16,2,64,896]{3,2,1,0:T(8,128)(2,1)} %param.10, pred[16,32]{1,0:T(8,128)(4,1)S(1)} %copy.31, bf16[16,32,2,64]{3,2,1,0:T(2,128)(2,1)S(1)} %gather.10), kind=kOutput, calls=%fused_computation.4 | convolution fusion | flops 118423552 | bytes 7471616 | tf_op jit(solution)/shard_map/xbyd,xydv->xbyv/dot_general | solution.py:68
  121.9 2.8 %copy.35 = f32[16,32,2,896]{3,2,1,0:T(2,128)S(1)} copy(f32[16,32,2,896]{3,1,2,0:T(8,128)S(1)} %select_bitcast_fusion) | data formatting | bytes 7340032 | tf_op jit(solution)/shard_map/jit(_where)/select_n | solution.py:71
  124.7 2.0 %copy.36 = f32[64,8,2,896]{3,1,2,0:T(8,128)} copy(f32[64,8,2,896]{3,2,1,0:T(2,128)S(1)} %bitcast.29) | data formatting | bytes 7340032
  126.7 8.2 %scatter_custom_fusion.1 = f32[128,1792]{1,0:T(8,128)S(1)} fusion(s32[512]{0:T(512)S(1)} %bitcast.35, f32[512,1792]{1,0:T(8,128)} %bitcast.30, f32[]{:T(128)} %constant.10.clone.1), kind=kCustom, calls=%fused_computation.12 | custom fusion | flops 917504 | bytes 918016 | tf_op jit(solution)/shard_map/scatter-add | solution.py:77
  134.9 8.3 %convolution_add_fusion.1 = f32[128,896]{1,0:T(8,128)S(1)} fusion(bf16[128,8192]{1,0:T(8,128)(2,1)} %all-gather.2.cloned.1.call-done, bf16[8192,896]{1,0:T(8,128)(2,1)} %param.7, f32[128,1792]{1,0:T(8,128)S(1)} %scatter_custom_fusion.1), kind=kOutput, calls=%fused_computation.9 | convolution fusion | flops 1879162880 | bytes 17694720 | tf_op jit(solution)/shard_map/dot_general | solution.py:44
  143.3 8.3 %fusion.3 = bf16[128,896]{1,0:T(8,128)(2,1)} fusion(bf16[128,8192]{1,0:T(8,128)(2,1)S(1)} %copy-done.1, bf16[8192,896]{1,0:T(8,128)(2,1)} %param.8, f32[128,1792]{1,0:T(8,128)S(1)} %scatter_custom_fusion.1, f32[128,896]{1,0:T(8,128)S(1)} %convolution_add_fusion.1), kind=kOutput, calls=%fused_computation.10 | convolution fusion | flops 1879851008 | bytes 17924096 | tf_op jit(solution)/shard_map/dot_general | solution.py:45
  (24 shorter events, 0.6 us)
Async XLA Ops:
  6.5 50.3 %copy-start = (bf16[1,8192,128]{2,1,0:T(8,128)(2,1)S(1)}, bf16[1,8192,128]{2,1,0:T(8,128)(2,1)}, u32[]{:S(2)}) copy-start(bf16[1,8192,128]{2,1,0:T(8,128)(2,1)} %param.9) | copy-start | bytes 6291460
  6.5 47.1 %all-gather.2.cloned.1.call-start = ((), (), s32[]{:S(2)}) async-start(), calls=%async_computation | async-start | bytes 2228224 | tf_op jit(solution)/shard_map/all_gather | solution.py:43
  134.9 8.3 %copy-start.1 = (bf16[128,8192]{1,0:T(8,128)(2,1)S(1)}, bf16[128,8192]{1,0:T(8,128)(2,1)}, u32[]{:S(2)}) copy-start(bf16[128,8192]{1,0:T(8,128)(2,1)} %all-gather.2.cloned.1.call-done) | copy-start | bytes 6291460
Sparse Core Ops, SparseCore 0:
  9.5 44.0 all-gather.1
where the time goes:
time: 159 us; the launch traced here: 158 us
  blocking collectives  73.3 us (46%)
  waiting for transfers between devices  28.5 us (18%)
  matrix products  19.9 us (13%)
  between operations  14.2 us (9%)
  local copies, waits for them, and re-layouts  12.5 us (8%)
  other arithmetic  10.1 us (6%)
    psum x1, blocking collectives, local(): reduced_rank = lax.psum(dense, 'tensor').astype(jnp.bfloat16)  59.6 us
    all_gather x1, waiting for transfers between devices, local(): collected_rows = lax.all_gather(tokens, 'tensor', axis=0, tiled=True)  27.8 us
    unnamed x1, blocking collectives  13.7 us
    dot_general x1, matrix products, local(): jnp.dot(collected_rows, up_matrix, preferred_element_type=jnp.float32)  8.31 us
    dot_general x1, matrix products, local(): jnp.dot(collected_rows, gate_matrix, preferred_element_type=jnp.float32)  8.3 us
    scatter-add x1, other arithmetic, local(): adapter_terms = jnp.zeros((total_rows, 2 * hidden_local), jnp.float32).at...  8.2 us
    unnamed x8, local copies, waits for them, and re-layouts  4.04 us
    gather x1, local copies, waits for them, and re-layouts, local(): collected_rows[local_token_rows[0]]  3.2 us
  transfers between devices with their start and end apart: 1, of which 1 were waited for; matrix products, arithmetic and copies ran while one was open for 3% of the time, Pallas kernels for 0%

commit v1 on v0

v1 whole, which is shorter than its diff:
```python
import functools

import jax
import jax.numpy as jnp
from jax import lax
from jax.experimental import pallas as pl
from jax.experimental.pallas import tpu as pltpu
from jax.sharding import PartitionSpec as P

SEQ = 4
MOST = 8
LANES = 128
MESH = pl.DeviceIdType.MESH
F32 = jnp.float32
BF16 = jnp.bfloat16


def plan(chips, chunk):
    far, near = chips // 2, chips - 1 - chips // 2
    return (far, near) if chunk % 2 == 0 else (near, far)


def pieces_of(width):
    pieces = []
    full = width // 256 * 256 if width >= 256 else 0
    for which in (0, 1):
        for start in range(0, full, 256):
            pieces.append([(which, start, 256)])
    if width > full:
        if (width - full) % LANES == 0:
            pieces.append([(0, full, width - full), (1, full, width - full)])
        else:
            pieces.append([(0, full, width - full)])
            pieces.append([(1, full, width - full)])
    return pieces


def kernel(
    n, chunks, fold,
    req, tok, gate, up, amap, bmap, out,
    xall, xs, gv, uv, av, bg, bu, acc, accl, packed, lg, lu,
    tok_sem, w_sem, b_sem, ring_send, ring_recv, sib_send, sib_recv, low_send, low_recv,
):
    depth, width = gate.shape
    own_rows = tok.shape[0]
    rows = n * own_rows
    slots = MOST * SEQ
    chips = n // 2
    kc = depth // chunks
    rank = bmap.shape[2]
    per = LANES // rank
    me = lax.axis_index("tensor")
    core = me % 2
    chip = me // 2

    def chip_at(p):
        p = (p + chips) % chips
        if not fold:
            return p
        y = p // (chips // 2)
        return 2 * (p + y * (chips - 1 - 2 * p)) + y

    if fold:
        pos = chip // 2 + (chip % 2) * (chips - 1 - 2 * (chip // 2))
    else:
        pos = chip
    right = chip_at(pos + 1) * 2 + core
    left = chip_at(pos - 1) * 2 + core
    sib = me + 1 - 2 * core

    def columns(c):
        return pl.ds(0, LANES + kc) if c == 0 else pl.ds(LANES + c * kc, kc)

    def weights(c):
        span = pl.ds(c * kc, kc)
        return [
            pltpu.make_async_copy(amap.at[0, span], av.at[span], w_sem.at[c, 0]),
            pltpu.make_async_copy(gate.at[span], gv.at[span], w_sem.at[c, 1]),
            pltpu.make_async_copy(up.at[span], uv.at[span], w_sem.at[c, 2]),
        ]

    out_maps = [
        pltpu.make_async_copy(bmap.at[:, 0], bg, b_sem.at[0]),
        pltpu.make_async_copy(bmap.at[:, 1], bu, b_sem.at[1]),
    ]
    own_copy = pltpu.make_async_copy(tok, xall.at[me, :, pl.ds(LANES, depth)], tok_sem)
    own_copy.start()
    for copy in weights(0) + (weights(1) if chunks > 1 else []):
        copy.start()

    barrier = pltpu.get_barrier_semaphore()
    for off in range(1, n):
        pl.semaphore_signal(barrier, inc=1, device_id={"tensor": (me + off) % n}, device_id_type=MESH)

    row_of = lax.broadcasted_iota(jnp.int32, (own_rows, LANES), 0) // SEQ
    ids = jnp.zeros((own_rows, LANES), jnp.int32)
    for r in range(own_rows // SEQ):
        ids = jnp.where(row_of == r, req[r, 0], ids)
    xall[me, :, 0:LANES] = ids.astype(F32).astype(BF16)
    acc[...] = jnp.zeros_like(acc)
    accl[...] = jnp.zeros_like(accl)
    pl.semaphore_wait(barrier, n - 1)
    own_copy.wait()

    def block(owner, c):
        return xall.at[owner, :, columns(c)]

    def to_ring(way, c, s):
        owner = chip_at(pos - s if way == 0 else pos + s) * 2 + core
        return pltpu.make_async_remote_copy(
            src_ref=block(owner, c), dst_ref=block(owner, c),
            send_sem=ring_send.at[way, c, s], recv_sem=ring_recv.at[way, c, s],
            device_id={"tensor": right if way == 0 else left}, device_id_type=MESH,
        )

    def from_ring(way, c, s):
        owner = chip_at(pos - s - 1 if way == 0 else pos + s + 1) * 2 + core
        return pltpu.make_async_remote_copy(
            src_ref=block(owner, c), dst_ref=block(owner, c),
            send_sem=ring_send.at[way, c, s], recv_sem=ring_recv.at[way, c, s],
            device_id={"tensor": right if way == 0 else left}, device_id_type=MESH,
        )

    def to_sib(c, hop, whose):
        owner = chip_at(pos + hop) * 2 + whose
        return pltpu.make_async_remote_copy(
            src_ref=block(owner, c), dst_ref=block(owner, c),
            send_sem=sib_send.at[c, hop % chips], recv_sem=sib_recv.at[c, hop % chips],
            device_id={"tensor": sib}, device_id_type=MESH,
        )

    sent = []

    def go(copy):
        copy.start()
        sent.append(copy)

    def ring_step(c, s):
        ways = plan(chips, c)
        if s == 0:
            for way in (0, 1):
                if ways[way] > 0:
                    go(to_ring(way, c, 0))
            go(to_sib(c, 0, core))
            return
        for way in (0, 1):
            if s <= ways[way]:
                from_ring(way, c, s - 1).wait_recv()
                if s < ways[way]:
                    go(to_ring(way, c, s))
        for way in (0, 1):
            if s <= ways[way]:
                go(to_sib(c, -s if way == 0 else s, core))

    def gather_sib(c):
        ways = plan(chips, c)
        for hop in range(-ways[0], ways[1] + 1):
            to_sib(c, hop, 1 - core).wait_recv()

    def lay(c):
        base = LANES + c * kc
        xs[c % 2] = xall[:, :, base:base + kc].astype(F32).reshape(rows, kc).astype(BF16)

    pieces = pieces_of(width)

    def low_part(c):
        accl[...] += jnp.dot(xs[c % 2], av[c * kc:(c + 1) * kc], preferred_element_type=F32)

    def main_part(c):
        for i, piece in enumerate(pieces):
            cols = [
                (gv, uv)[which][c * kc:(c + 1) * kc, start:start + size]
                for which, start, size in piece
            ]
            w = cols[0] if len(cols) == 1 else jnp.concatenate(cols, axis=1)
            size = sum(part[2] for part in piece)
            acc[i, :, 0:size] += jnp.dot(xs[c % 2], w, preferred_element_type=F32)

    steps = max(plan(chips, 0))
    done = -1
    for tick in range(chunks + steps):
        for c in range(chunks):
            s = tick - c
            if 0 <= s <= steps:
                ring_step(c, s)
        ready = tick - steps - 1
        if ready >= 0:
            gather_sib(ready)
            lay(ready)
            for copy in weights(ready):
                copy.wait()
            low_part(ready)
            if ready < chunks - 2:
                main_part(ready)
        nxt = ready + 2
        if ready >= 0 and nxt < chunks:
            for copy in weights(nxt):
                copy.start()
        if nxt == chunks - 1:
            for copy in out_maps:
                copy.start()

    last = chunks - 1
    gather_sib(last)
    lay(last)
    for copy in weights(last):
        copy.wait()
    low_part(last)

    idw = xall[:, :, 0:LANES].astype(F32).reshape(rows, LANES)
    idc = idw[:, 0:1]
    idr = idw.T[0:1, :]
    same = idc == idr
    at_row = lax.broadcasted_iota(jnp.int32, (rows, rows), 0)
    at_col = lax.broadcasted_iota(jnp.int32, (rows, rows), 1)
    place_r = jnp.sum(jnp.where(same & (at_row < at_col), 1.0, 0.0), axis=0, keepdims=True)
    dest_r = (idr * slots + place_r).astype(jnp.int32)
    slot_of = lax.broadcasted_iota(jnp.int32, (slots, rows), 0) + me * slots
    pick = jnp.where(slot_of == dest_r, 1.0, 0.0).astype(BF16)
    low_own = accl[...].astype(BF16)
    packed[me] = jnp.dot(pick, low_own, preferred_element_type=F32).astype(BF16)

    def low_copy(off, owner):
        return pltpu.make_async_remote_copy(
            src_ref=packed.at[owner], dst_ref=packed.at[owner],
            send_sem=low_send.at[off], recv_sem=low_recv.at[off],
            device_id={"tensor": (me + off) % n}, device_id_type=MESH,
        )

    for off in range(1, n):
        go(low_copy(off, me))

    if chunks > 1:
        main_part(last - 1)
    main_part(last)
    place_c = jnp.sum(jnp.where(same & (at_col < at_row), 1.0, 0.0), axis=1, keepdims=True)
    dest_c = (idc * slots + place_c).astype(jnp.int32)
    spread = jnp.where(
        lax.broadcasted_iota(jnp.int32, (rows, n * slots), 1) == dest_c, 1.0, 0.0
    ).astype(BF16)
    for copy in out_maps:
        copy.wait()
    for off in range(1, n):
        low_copy(off, (me - off + n) % n).wait_recv()
    low = jnp.dot(spread, packed[...].reshape(n * slots, LANES), preferred_element_type=F32)
    idi = idc.astype(jnp.int32)
    group = lax.broadcasted_iota(jnp.int32, (rows, LANES), 1) // rank
    for which, dst in ((0, lg), (1, lu)):
        part = low[:, which * rank:(which + 1) * rank]
        twice = jnp.concatenate([part] * per, axis=1)
        for j in range(n // per):
            dst[:, j * LANES:(j + 1) * LANES] = jnp.where(
                group + j * per == idi, twice, 0.0
            ).astype(BF16)

    where_is = {}
    for i, piece in enumerate(pieces):
        offset = 0
        for which, start, size in piece:
            where_is[which, start] = (i, offset, size)
            offset += size
    for (which, start), (i, offset, size) in list(where_is.items()):
        if which:
            continue
        totals = []
        for kind, left_side, maps in ((0, lg, bg), (1, lu, bu)):
            j, off, _ = where_is[kind, start]
            totals.append(
                acc[j, :, off:off + size]
                + jnp.dot(
                    left_side[...],
                    maps[:, :, start:start + size].reshape(n * rank, size),
                    preferred_element_type=F32,
                )
            )
        g, u = totals
        out[:, start:start + size] = (g / (1.0 + jnp.exp(-g)) * u).astype(out.dtype)

    for copy in sent:
        copy.wait_send()


def local(tokens, gate_matrix, up_matrix, adapter_input_maps, adapter_output_maps, request_adapter):
    n = lax.axis_size("tensor")
    depth, width = gate_matrix.shape
    own_rows = tokens.shape[0]
    rows = n * own_rows
    rank = adapter_output_maps.shape[2]
    chips = n // 2
    chunks = 4
    kc = depth // chunks
    steps = chips // 2 + 1
    pieces = pieces_of(width)
    wide = max(sum(part[2] for part in piece) for piece in pieces)
    dma = pltpu.SemaphoreType.DMA
    anyspace = pl.BlockSpec(memory_space=pl.ANY)
    flops = 2 * rows * depth * (2 * width + 2 * rank)
    return pl.pallas_call(
        functools.partial(kernel, n, chunks, chips == 8),
        out_shape=jax.ShapeDtypeStruct((rows, width), BF16),
        in_specs=[pl.BlockSpec(memory_space=pltpu.SMEM)] + [anyspace] * 5,
        out_specs=pl.BlockSpec(memory_space=pltpu.VMEM),
        scratch_shapes=[
            pltpu.VMEM((n, own_rows, LANES + depth), BF16),
            pltpu.VMEM((2, rows, kc), BF16),
            pltpu.VMEM((depth, width), BF16),
            pltpu.VMEM((depth, width), BF16),
            pltpu.VMEM((depth, LANES), BF16),
            pltpu.VMEM((n, rank, width), BF16),
            pltpu.VMEM((n, rank, width), BF16),
            pltpu.VMEM((len(pieces), rows, wide), F32),
            pltpu.VMEM((rows, LANES), F32),
            pltpu.VMEM((n, MOST * SEQ, LANES), BF16),
            pltpu.VMEM((rows, n * rank), BF16),
            pltpu.VMEM((rows, n * rank), BF16),
            dma,
            dma((chunks, 3)),
            dma((2,)),
            dma((2, chunks, steps)),
            dma((2, chunks, steps)),
            dma((chunks, chips)),
            dma((chunks, chips)),
            dma((n,)),
            dma((n,)),
        ],
        compiler_params=pltpu.CompilerParams(
            collective_id=0, has_side_effects=True, vmem_limit_bytes=60 * 1024 * 1024
        ),
        cost_estimate=pl.CostEstimate(
            flops=flops, bytes_accessed=4 * depth * width, transcendentals=rows * width
        ),
    )(request_adapter, tokens, gate_matrix, up_matrix, adapter_input_maps, adapter_output_maps)


def solution(mesh):
    in_specs = (
        P(("groups", "tensor"), None),
        P(None, "tensor"),
        P(None, "tensor"),
        P("tensor", None, None),
        P(None, None, None, "tensor"),
        P(("groups", "tensor"), None),
    )
    out_specs = P("groups", "tensor")
    return jax.shard_map(local, mesh=mesh, in_specs=in_specs, out_specs=out_specs, check_vma=False)
```

time: 159 us -> 44.4 us (0.28)
  blocking collectives: 73.3 us -> 0 us
  Pallas kernels: 0 us -> 41.2 us
  waiting for transfers between devices: 28.5 us -> 0 us
  matrix products: 19.9 us -> 0 us
  between operations: 14.2 us -> 0.01 us
  other arithmetic: 10.1 us -> 0 us
  local copies, waits for them, and re-layouts: 12.5 us -> 2.94 us
    psum x1 -> x0, blocking collectives: 59.6 us -> none  [local(): reduced_rank = lax.psum(dense, 'tensor').astype(jnp.bfloat16)]
    pallas_call x0 -> x1, Pallas kernels: none -> 41.2 us  [local(): pl.pallas_call(functools.partial(kernel, n, chunks, chips == 8), out_shap...]
    all_gather x1 -> x0, waiting for transfers between devices: 27.8 us -> none  [local(): collected_rows = lax.all_gather(tokens, 'tensor', axis=0, tiled=True)]
    dot_general x4 -> x0, matrix products: 19.9 us -> none  [the longest x1 8.31 us: local(): jnp.dot(collected_rows, up_matrix, preferred_element_type=jnp.float32)]
    unnamed x1 -> x0, blocking collectives: 13.7 us -> none
    scatter-add x2 -> x0, other arithmetic: 8.93 us -> none  [the longest x1 8.2 us: local(): adapter_terms = jnp.zeros((total_rows, 2 * hidden_local), jnp.float32).at...]
    gather x3 -> x0, local copies, waits for them, and re-layouts: 4.67 us -> none  [the longest x1 3.2 us: local(): collected_rows[local_token_rows[0]]]
    select_n x3 -> x0, local copies, waits for them, and re-layouts: 2.98 us -> none  [the longest x1 2.83 us: local(): jnp.where(live[:, :, None, None], slot_terms, 0.0)]
  transfers between devices with their start and end apart: 1 -> 0, of which waited for: 1 -> 0; matrix products, arithmetic and copies ran while one was open for 3% -> 0% of each run, Pallas kernels for 0% -> 0%
where the time goes in v1:
time: 44.4 us; the launch traced here: 44.1 us
  Pallas kernels  41.2 us (93%)
  local copies, waits for them, and re-layouts  2.94 us (7%)
    pallas_call x1, Pallas kernels, local(): pl.pallas_call(functools.partial(kernel, n, chunks, chips == 8), out_shap...  41.2 us
    unnamed x2, local copies, waits for them, and re-layouts  2.94 us

profile of v1, /device:TPU:0, one launch (start us, length us, event | category | flops | bytes accessed | tf_op | source)
XLA Modules:
  0.0 44.1 jit_solution(15258566434377744654)
XLA Ops:
  0.0 1.3 %copy.7.req = s32[2,1]{1,0:T(2,128)} copy(s32[2,1]{0,1:T(1,128)} %param.11) | data formatting | bytes 16 | tf_op args[5]
  1.3 41.2 %shard_map.64 = bf16[128,896]{1,0:T(8,128)(2,1)} custom-call(s32[2,1]{1,0:T(2,128)} %copy.7.req, bf16[8,8192]{1,0:T(8,128)(2,1)} %tok.1, bf16[8192,896]{1,0:T(8,128)(2,1)} %gate.1, bf16[8192,896]{1,0:T(8,128)(2,1)} %up.1, bf16[1,8192,128]{2,1,0:T(8,128)(2,1)} %amap.1, bf16[16,2,64,896]{3,2,1,0:T(8,128)(2,1)} %bmap.1), custom_call_target="tpu_custom_call" | custom-call | flops 4026531840 | bytes 29360128 | tf_op jit(solution)/shard_map/pallas_call | solution.py:298
  42.5 1.6 %copy.9 = bf16[128,896]{1,0:T(8,128)(2,1)} copy(bf16[128,896]{1,0:T(8,128)(2,1)} %shard_map.64) | data formatting | bytes 458752

commit v2 on v1

v2 whole, which is shorter than its diff:
```python
import functools

import jax
import jax.numpy as jnp
from jax import lax
from jax.experimental import pallas as pl
from jax.experimental.pallas import tpu as pltpu
from jax.sharding import PartitionSpec as P

SEQ = 4
MOST = 8
LANES = 128
MESH = pl.DeviceIdType.MESH
F32 = jnp.float32
BF16 = jnp.bfloat16


def pieces_of(width):
    pieces = []
    full = width // 256 * 256 if width >= 256 else 0
    for which in (0, 1):
        for start in range(0, full, 256):
            pieces.append([(which, start, 256)])
    if width > full:
        if (width - full) % LANES == 0:
            pieces.append([(0, full, width - full), (1, full, width - full)])
        else:
            pieces.append([(0, full, width - full)])
            pieces.append([(1, full, width - full)])
    return pieces


def kernel(
    n, chunks, ny,
    req, tok, gate, up, amap, bmap, out,
    xall, xs, gv, uv, av, bg, bu, acc, accl, packed, lg, lu,
    tok_sem, w_sem, b_sem, z_send, z_recv, y_send, y_recv, sib_send, sib_recv,
    low_send, low_recv, pair_send, pair_recv,
):
    depth, width = gate.shape
    own_rows = tok.shape[0]
    rows = n * own_rows
    slots = MOST * SEQ
    chips = n // 2
    kc = depth // chunks
    rank = bmap.shape[2]
    per = LANES // rank
    me = lax.axis_index("tensor")
    core = me % 2
    nz = n // (2 * ny)
    y, z = (me // 2) % ny, me // (2 * ny)

    def device(zz, yy, cc):
        return (zz * ny + yy) * 2 + cc

    order = [(d % 2, (d // 2) % ny, d // (2 * ny)) for d in range(n)]
    sib = me + 1 - 2 * core

    def columns(c):
        return pl.ds(0, LANES + kc) if c == 0 else pl.ds(LANES + c * kc, kc)

    def weights(c):
        span = pl.ds(c * kc, kc)
        return [
            pltpu.make_async_copy(amap.at[0, span], av.at[span], w_sem.at[c, 0]),
            pltpu.make_async_copy(gate.at[span], gv.at[span], w_sem.at[c, 1]),
            pltpu.make_async_copy(up.at[span], uv.at[span], w_sem.at[c, 2]),
        ]

    out_maps = [
        pltpu.make_async_copy(bmap.at[:, 0], bg, b_sem.at[0]),
        pltpu.make_async_copy(bmap.at[:, 1], bu, b_sem.at[1]),
    ]
    own_copy = pltpu.make_async_copy(tok, xall.at[core, y, z, :, pl.ds(LANES, depth)], tok_sem)
    own_copy.start()

    barrier = pltpu.get_barrier_semaphore()
    peers = [
        (dz, dy) for dz in range(nz) for dy in range(ny) if dz or dy
    ]

    def peer(dz, dy):
        return (z + dz) % nz, (y + dy) % ny

    for dz, dy in peers:
        pl.semaphore_signal(
            barrier, inc=1, device_id={"tensor": device(*peer(dz, dy), core)}, device_id_type=MESH
        )
    pl.semaphore_signal(barrier, inc=1, device_id={"tensor": sib}, device_id_type=MESH)

    row_of = lax.broadcasted_iota(jnp.int32, (own_rows, LANES), 0) // SEQ
    ids = jnp.zeros((own_rows, LANES), jnp.int32)
    for r in range(own_rows // SEQ):
        ids = jnp.where(row_of == r, req[0, r], ids)
    xall[core, y, z, :, 0:LANES] = ids.astype(F32).astype(BF16)
    acc[...] = jnp.zeros_like(acc)
    accl[...] = jnp.zeros_like(accl)
    pl.semaphore_wait(barrier, len(peers) + 1)
    own_copy.wait()

    def remote(ref, send, recv, target):
        return pltpu.make_async_remote_copy(
            src_ref=ref, dst_ref=ref, send_sem=send, recv_sem=recv,
            device_id={"tensor": target}, device_id_type=MESH,
        )

    sent = []

    def go(copy):
        copy.start()
        sent.append(copy)

    def z_copy(c, dz, zz):
        ref = xall.at[core, y, zz, :, columns(c)]
        return remote(ref, z_send.at[c, dz], z_recv.at[c, dz], device((z + dz) % nz, y, core))

    def y_copy(c, yy, dz):
        ref = xall.at[core, yy, (z - dz + nz) % nz, :, columns(c)]
        return remote(ref, y_send.at[c, dz], y_recv.at[c, dz], device(z, (y + 1) % ny, core))

    def sib_copy(c, cc, dy):
        ref = xall.at[cc, (y + dy) % ny, :, :, columns(c)]
        return remote(ref, sib_send.at[c, dy], sib_recv.at[c, dy], sib)

    def stage_z(c):
        for dz in range(1, nz):
            z_copy(c, dz, (z - dz + nz) % nz).wait_recv()
            if ny > 1:
                go(y_copy(c, y, dz))
        go(sib_copy(c, core, 0))

    def stage_y(c):
        if ny > 1:
            for dz in range(nz):
                y_copy(c, (y + 1) % ny, dz).wait_recv()
            go(sib_copy(c, core, 1))

    def gather_sib(c):
        for dy in range(ny):
            sib_copy(c, 1 - core, dy).wait_recv()

    def rows_of(cols):
        return jnp.concatenate([xall[k, i, j, :, cols].astype(F32) for k, i, j in order], axis=0)

    def lay(c):
        base = LANES + c * kc
        xs[c % 2] = rows_of(slice(base, base + kc)).astype(BF16)

    pieces = pieces_of(width)

    def low_part(c):
        accl[...] += jnp.dot(xs[c % 2], av[c * kc:(c + 1) * kc], preferred_element_type=F32)

    def main_part(c, first=0, stop=None):
        for i, piece in list(enumerate(pieces))[first:stop]:
            cols = [
                (gv, uv)[which][c * kc:(c + 1) * kc, start:start + size]
                for which, start, size in piece
            ]
            w = cols[0] if len(cols) == 1 else jnp.concatenate(cols, axis=1)
            size = sum(part[2] for part in piece)
            acc[i, :, 0:size] += jnp.dot(xs[c % 2], w, preferred_element_type=F32)

    for c in range(chunks):
        for dz in range(1, nz):
            go(z_copy(c, dz, z))
        if ny > 1:
            go(y_copy(c, y, 0))
    for copy in weights(0) + (weights(1) if chunks > 1 else []):
        copy.start()
    for tick in range(chunks + 1):
        if tick < chunks:
            stage_z(tick)
        if 1 <= tick:
            stage_y(tick - 1)
        ready = tick - 2
        if ready >= 0:
            gather_sib(ready)
            lay(ready)
            for copy in weights(ready):
                copy.wait()
            low_part(ready)
            main_part(ready)
        nxt = ready + 2
        if ready >= 0 and nxt < chunks:
            for copy in weights(nxt):
                copy.start()
        if nxt == max(chunks - 1, 1):
            for copy in out_maps:
                copy.start()

    last = chunks - 1
    idw = rows_of(slice(0, LANES))
    idc = idw[:, 0:1]
    idr = idw.T[0:1, :]
    same = idc == idr
    at_row = lax.broadcasted_iota(jnp.int32, (rows, rows), 0)
    at_col = lax.broadcasted_iota(jnp.int32, (rows, rows), 1)
    place_r = jnp.sum(jnp.where(same & (at_row < at_col), 1.0, 0.0), axis=0, keepdims=True)
    dest_r = (idr * slots + place_r).astype(jnp.int32)
    slot_of = lax.broadcasted_iota(jnp.int32, (slots, rows), 0) + me * slots
    pick = jnp.where(slot_of == dest_r, 1.0, 0.0).astype(BF16)
    place_c = jnp.sum(jnp.where(same & (at_col < at_row), 1.0, 0.0), axis=1, keepdims=True)
    dest_c = (idc * slots + place_c).astype(jnp.int32)
    spread = jnp.where(
        lax.broadcasted_iota(jnp.int32, (rows, n * slots), 1) == dest_c, 1.0, 0.0
    ).astype(BF16)
    idi = idc.astype(jnp.int32)
    group = lax.broadcasted_iota(jnp.int32, (rows, LANES), 1) // rank
    gather_sib(last)
    lay(last)
    for copy in weights(last):
        copy.wait()
    low_part(last)

    low_own = accl[...].astype(BF16)
    packed[core, y, z] = jnp.dot(pick, low_own, preferred_element_type=F32).astype(BF16)

    def low_copy(i, zz, yy):
        dz, dy = peers[i]
        ref = packed.at[core, yy, zz]
        return remote(ref, low_send.at[i], low_recv.at[i], device(*peer(dz, dy), core))

    for i in range(len(peers)):
        go(low_copy(i, z, y))
    early = len(pieces) // 2
    main_part(last, 0, early)
    for i, (dz, dy) in enumerate(peers):
        low_copy(i, (z - dz + nz) % nz, (y - dy + ny) % ny).wait_recv()

    def pair_copy(cc):
        return remote(packed.at[cc], pair_send, pair_recv, sib)

    go(pair_copy(core))
    main_part(last, early, len(pieces))
    for copy in out_maps:
        copy.wait()
    pair_copy(1 - core).wait_recv()
    table = jnp.concatenate([packed[k, i, j] for k, i, j in order], axis=0)
    low = jnp.dot(spread, table, preferred_element_type=F32)
    for which, dst in ((0, lg), (1, lu)):
        part = low[:, which * rank:(which + 1) * rank]
        twice = jnp.concatenate([part] * per, axis=1)
        for j in range(n // per):
            dst[:, j * LANES:(j + 1) * LANES] = jnp.where(
                group + j * per == idi, twice, 0.0
            ).astype(BF16)

    where_is = {}
    for i, piece in enumerate(pieces):
        offset = 0
        for which, start, size in piece:
            where_is[which, start] = (i, offset, size)
            offset += size
    for (which, start), (i, offset, size) in list(where_is.items()):
        if which:
            continue
        totals = []
        for kind, left_side, maps in ((0, lg, bg), (1, lu, bu)):
            j, off, _ = where_is[kind, start]
            totals.append(
                acc[j, :, off:off + size]
                + jnp.dot(
                    left_side[...],
                    maps[:, :, start:start + size].reshape(n * rank, size),
                    preferred_element_type=F32,
                )
            )
        g, u = totals
        out[:, start:start + size] = (g / (1.0 + jnp.exp(-g)) * u).astype(out.dtype)

    for copy in sent:
        copy.wait_send()


def local(tokens, gate_matrix, up_matrix, adapter_input_maps, adapter_output_maps, request_adapter):
    n = lax.axis_size("tensor")
    depth, width = gate_matrix.shape
    own_rows = tokens.shape[0]
    rows = n * own_rows
    rank = adapter_output_maps.shape[2]
    chips = n // 2
    chunks = 4
    kc = depth // chunks
    ny = 2 if chips == 8 else 1
    nz = chips // ny
    pieces = pieces_of(width)
    wide = max(sum(part[2] for part in piece) for piece in pieces)
    dma = pltpu.SemaphoreType.DMA
    anyspace = pl.BlockSpec(memory_space=pl.ANY)
    flops = 2 * rows * depth * (2 * width + 2 * rank)
    return pl.pallas_call(
        functools.partial(kernel, n, chunks, ny),
        out_shape=jax.ShapeDtypeStruct((rows, width), BF16),
        in_specs=[pl.BlockSpec(memory_space=pltpu.SMEM)] + [anyspace] * 5,
        out_specs=pl.BlockSpec(memory_space=pltpu.VMEM),
        scratch_shapes=[
            pltpu.VMEM((2, ny, nz, own_rows, LANES + depth), BF16),
            pltpu.VMEM((2, rows, kc), BF16),
            pltpu.VMEM((depth, width), BF16),
            pltpu.VMEM((depth, width), BF16),
            pltpu.VMEM((depth, LANES), BF16),
            pltpu.VMEM((n, rank, width), BF16),
            pltpu.VMEM((n, rank, width), BF16),
            pltpu.VMEM((len(pieces), rows, wide), F32),
            pltpu.VMEM((rows, LANES), F32),
            pltpu.VMEM((2, ny, nz, MOST * SEQ, LANES), BF16),
            pltpu.VMEM((rows, n * rank), BF16),
            pltpu.VMEM((rows, n * rank), BF16),
            dma,
            dma((chunks, 3)),
            dma((2,)),
            dma((chunks, nz)),
            dma((chunks, nz)),
            dma((chunks, nz)),
            dma((chunks, nz)),
            dma((chunks, ny)),
            dma((chunks, ny)),
            dma((chips,)),
            dma((chips,)),
            dma,
            dma,
        ],
        compiler_params=pltpu.CompilerParams(
            collective_id=0, has_side_effects=True, vmem_limit_bytes=60 * 1024 * 1024
        ),
        cost_estimate=pl.CostEstimate(
            flops=flops, bytes_accessed=4 * depth * width, transcendentals=rows * width
        ),
    )(request_adapter.T, tokens, gate_matrix, up_matrix, adapter_input_maps, adapter_output_maps)


def solution(mesh):
    in_specs = (
        P(("groups", "tensor"), None),
        P(None, "tensor"),
        P(None, "tensor"),
        P("tensor", None, None),
        P(None, None, None, "tensor"),
        P(("groups", "tensor"), None),
    )
    out_specs = P("groups", "tensor")
    return jax.shard_map(local, mesh=mesh, in_specs=in_specs, out_specs=out_specs, check_vma=False)
```

time: 44.4 us -> 39.1 us (0.88)
  Pallas kernels: 41.2 us -> 37.2 us
  local copies, waits for them, and re-layouts: 2.94 us -> 1.65 us
    pallas_call x1, Pallas kernels: 41.2 us -> 37.2 us  [local(): pl.pallas_call(functools.partial(kernel, n, chunks, ny), out_shape=jax.Sh...]
    unnamed x2 -> x1, local copies, waits for them, and re-layouts: 2.94 us -> 1.65 us
where the time goes in v2:
time: 39.1 us; the launch traced here: 38.8 us
  Pallas kernels  37.2 us (95%)
  local copies, waits for them, and re-layouts  1.65 us (4%)
    pallas_call x1, Pallas kernels, local(): pl.pallas_call(functools.partial(kernel, n, chunks, ny), out_shape=jax.Sh...  37.2 us
    unnamed x1, local copies, waits for them, and re-layouts  1.65 us

profile of v2, /device:TPU:0, one launch (start us, length us, event | category | flops | bytes accessed | tf_op | source)
XLA Modules:
  0.0 38.8 jit_solution(8873987983317227938)
XLA Ops:
  0.0 37.2 %shard_map.64 = bf16[128,896]{1,0:T(8,128)(2,1)} custom-call(s32[1,2]{1,0:T(1,128)} %bitcast.1, bf16[8,8192]{1,0:T(8,128)(2,1)} %tok.1, bf16[8192,896]{1,0:T(8,128)(2,1)} %gate.1, bf16[8192,896]{1,0:T(8,128)(2,1)} %up.1, bf16[1,8192,128]{2,1,0:T(8,128)(2,1)} %amap.1, bf16[16,2,64,896]{3,2,1,0:T(8,128)(2,1)} %bmap.1), custom_call_target="tpu_custom_call" | custom-call | flops 4026531840 | bytes 29360128 | tf_op jit(solution)/shard_map/pallas_call | solution.py:292
  37.2 1.6 %copy.8 = bf16[128,896]{1,0:T(8,128)(2,1)} copy(bf16[128,896]{1,0:T(8,128)(2,1)} %shard_map.64) | data formatting | bytes 458752
